TPU v7x, 32 devices: a whole 2x2x4 slice. The times are simulated.
32 devices in a mesh: sector: 4 (over x, core), tile: 8 (over z, y).
Axes of the slice: x: 2, y: 2, z: 4, core: 2. Of those that a mesh axis runs over, the one named last changes fastest.
Arguments:
- snapshots: bfloat16 [4, 30720, 384], P(None, ('sector', 'tile')), may hold values from -6 to 6
- density: float32 [30720], P(('sector', 'tile')), may hold values from 0.5 to 2
- sound_speed: float32 [30720], P(('sector', 'tile')), may hold values from 0.5 to 2
- offsets: int32 [30720], P(('sector', 'tile')), may hold values from -32 to 32
- rotation: bfloat16 [384, 128], P('tile'), may hold values from -0.3125 to 0.3125
Outputs:
- projection: float32 [4, 384, 128], replicated
All inputs are finite; a program needn't handle non-finite values.
Results may differ from a plain program's by a relative error of at most 0.0003.
Values may be sent and summed in bfloat16 or wider, within the bound.
A program may use at most 64 MiB of HBM per device.

v0:
```python
import math

import jax
import jax.numpy as jnp
from jax import lax
from jax.sharding import PartitionSpec as P

HALO = 32


def padded_2(block, sides, width):
    for axis, dim in sides:
        count = lax.axis_size(axis)
        forward = [(i, i + 1) for i in range(count - 1)]
        forward.append((count - 1, 0))
        backward = [(target, source) for source, target in forward]
        low = lax.ppermute(
            lax.slice_in_dim(block, block.shape[dim] - width, None, axis=dim), axis, forward
        )
        high = lax.ppermute(lax.slice_in_dim(block, 0, width, axis=dim), axis, backward)
        block = jnp.concatenate([low, block, high], axis=dim)
    return block


def weighting(local_cells, near_press, near_sum, density, sound_speed):
    local_wide = local_cells.astype(jnp.float32)
    inverse = 1.0 / (density * sound_speed * sound_speed)
    vel_local = local_wide[1] + local_wide[2] + local_wide[3]
    potential = local_wide[0] * inverse + 0.5 * (near_sum - vel_local) / sound_speed
    kinetic = (
        density[None] * local_wide[1:]
        + 0.5 * (near_press - local_wide[0])[None] / sound_speed[None]
    )
    return jnp.concatenate([potential[None], kinetic], axis=0).astype(jnp.bfloat16)


def with_rims(field, extended):
    return jnp.concatenate(
        [extended[:, :HALO], field, extended[:, extended.shape[1] - HALO :]], axis=1
    )


def edge_rows(field, cell_count):
    return jnp.concatenate([field[:, :HALO], field[:, cell_count - HALO :]], axis=1)


def on_device(snapshots, density, sound_speed, offsets, rotation):
    cell_count = snapshots.shape[1]
    width_snap = snapshots.shape[2]
    neighbor_rows = jnp.arange(cell_count, dtype=jnp.int32) + offsets + HALO
    edges = edge_rows(snapshots, cell_count)
    extended = padded_2(edges, ((("sector", "tile"), 1),), HALO)
    padded = with_rims(snapshots, extended)
    neighbors = jnp.take(padded, neighbor_rows, axis=1).astype(jnp.float32)
    near_press = neighbors[0]
    near_sum = neighbors[1] + neighbors[2] + neighbors[3]
    weighted = weighting(snapshots, near_press, near_sum, density[:, None], sound_speed[:, None])
    full_rotation = lax.all_gather(rotation, "tile", axis=0, tiled=True)
    mode_count = full_rotation.shape[1]
    mode_fields = jnp.dot(
        snapshots.reshape(4 * cell_count, width_snap),
        full_rotation,
        preferred_element_type=jnp.float32,
    )
    mode_fields = mode_fields.astype(jnp.bfloat16).reshape(4, cell_count, mode_count)
    parts = [
        jnp.dot(weighted[component].T, mode_fields[component], preferred_element_type=jnp.float32)
        for component in range(4)
    ]
    partial_sum = jnp.stack(parts, axis=0)
    summed = lax.psum(partial_sum, ("sector", "tile"))
    cell_total = cell_count * lax.axis_size("sector") * lax.axis_size("tile")
    return summed / math.sqrt(cell_total)


def solution(mesh):
    return jax.shard_map(
        on_device,
        mesh=mesh,
        in_specs=(
            P(None, ("sector", "tile"), None),
            P(("sector", "tile")),
            P(("sector", "tile")),
            P(("sector", "tile")),
            P("tile", None),
        ),
        out_specs=P(),
        check_vma=False,
    )
```

profile of v0, /device:TPU:1, one launch (start us, length us, event | category | flops | bytes accessed | tf_op | source)
XLA Modules:
  0.0 229.3 jit_solution(10013859329396466280)
XLA Ops:
  6.5 0.0 all-reduce.2.cloned.1.call-start
  6.6 0.0 copy-start
  6.6 7.5 %fusion.21 = (bf16[4,960,384]{2,0,1:T(4,128)(2,1)S(1)}, f32[4,960,384]{2,0,1:T(4,128)}) fusion(bf16[4,960,384]{2,1,0:T(8,128)(2,1)} %param.5), kind=kLoop, calls=%fused_computation.44 | loop fusion | flops 1474560 | bytes 11796480 | tf_op args[0]
  14.1 0.1 fusion.20
  14.2 2.1 collective-permute-start
  16.3 3.7 %collective-permute-start.1 = (bf16[4,32,384]{2,0,1:T(4,128)(2,1)S(1)}, bf16[4,32,384]{2,0,1:T(4,128)(2,1)S(1)}, u32[]{:S(2)}, u32[]{:S(2)}) collective-permute-start(bf16[4,32,384]{2,0,1:T(4,128)(2,1)S(1)} %get-tuple-element.11), channel_id=1, source_target_pairs={{1,0},{2,1},{3,2},{4,3},{5,4},{6,5},{7,6},{8,7},{9,8},{10,9},{11,1... | collective-permute-start | bytes 294920 | tf_op jit(solution)/shard_map/ppermute | solution.py:20
  20.0 0.0 copy-done.3
  20.0 0.0 copy-done.4
  20.0 24.5 %all_gather.3 = bf16[384,128]{1,0:T(8,128)(2,1)S(1)} all-gather(bf16[48,128]{1,0:T(8,128)(2,1)S(1)} %copy-done.4), channel_id=1, replica_groups=mesh['sector'=4,'tile'=8] {'tile'}, dimensions={0}, use_global_device_ids=true | all-gather | bytes 110592 | tf_op jit(solution)/shard_map/all_gather | solution.py:58
  44.5 0.0 copy-done.2
  44.5 0.0 copy-done.1
  44.5 0.0 copy-done
  44.5 0.9 convolution_convert_fusion
  45.5 0.0 collective-permute-done
  45.5 0.0 collective-permute-done.1
  45.5 3.7 %pad_maximum_fusion = bf16[4,1024,384]{2,0,1:T(4,128)(2,1)} fusion(bf16[4,32,384]{2,0,1:T(4,128)(2,1)S(1)} %collective-permute-done.1, bf16[4,960,384]{2,0,1:T(4,128)(2,1)S(1)} %get-tuple-element.12, bf16[4,32,384]{2,0,1:T(4,128)(2,1)S(1)} %collective-permute-done), kind=kLoop, calls=%fused_computation.6 | loop fusion | flops 3145728 | bytes 6291456 | tf_op jit(solution)/shard_map/concatenate | solution.py:38
  49.2 11.9 %gather_fusion = bf16[960,4,384]{2,1,0:T(4,128)(2,1)} fusion(bf16[4,1024,384]{2,0,1:T(4,128)(2,1)} %pad_maximum_fusion, s32[1024]{0:T(1024)S(1)} %pad_clamp_fusion), kind=kCustom, calls=%fused_computation | custom fusion | bytes 5902080 | tf_op jit(solution)/shard_map/jit(_take)/gather | solution.py:54
  61.1 5.0 %convert_bitcast_fusion = f32[4,960,384]{2,0,1:T(4,128)S(1)} fusion(bf16[960,4,384]{2,1,0:T(4,128)(2,1)} %gather_fusion, pred[960]{0:T(1024)(128)(4,1)S(1)} %compare_and_fusion), kind=kLoop, calls=%fused_computation.4 | loop fusion | flops 2949120 | bytes 8848320 | tf_op jit(solution)/shard_map/convert_element_type | solution.py:54
  66.1 0.0 slice-done
  66.1 0.0 slice-done.1
  66.1 12.0 %fusion.5 = (bf16[1,960,384]{2,0,1:T(2,128)(2,1)S(1)}, f32[1,960,384]{2,0,1:T(1,128)S(1)}) fusion(f32[4,960,384]{2,0,1:T(4,128)S(1)} %bitcast.29, f32[4,960,384]{2,0,1:T(4,128)S(1)} %convert_bitcast_fusion, f32[960]{0:T(1024)S(1)} %fusion.18, f32[960]{0:T(1024)S(1)} %copy-done.1), kind=kLoop, calls=%fused_computation.17 | loop fusion | flops 4792320 | bytes 14016000 | tf_op jit(solution)/shard_map/slice | solution.py:67
  78.1 0.1 copy.38
  78.2 3.5 %fusion.1 = bf16[3,960,384]{2,0,1:T(4,128)(2,1)S(1)} fusion(f32[4,960,384]{2,0,1:T(4,128)S(1)} %bitcast.29, f32[960,384]{1,0:T(8,128)S(1)} %bitcast.31, f32[960]{0:T(1024)S(1)} %copy-done.2), kind=kLoop, calls=%fused_computation.3 | loop fusion | flops 3317760 | bytes 8113920 | tf_op jit(solution)/shard_map/convert.1
  81.8 3.2 %fusion.19 = (bf16[1,960,384]{2,0,1:T(2,128)(2,1)S(1)}, bf16[1,960,384]{2,0,1:T(2,128)(2,1)S(1)}, bf16[1,960,384]{2,0,1:T(2,128)(2,1)S(1)}) fusion(bf16[3,960,384]{2,0,1:T(4,128)(2,1)S(1)} %fusion.1), kind=kLoop, calls=%fused_computation.42 | loop fusion | bytes 4423680 | tf_op jit(solution)/shard_map/slice | solution.py:67
  85.0 0.4 convolution_bitcast_fusion
  85.4 0.4 convolution_bitcast_fusion.1
  85.8 0.4 convolution_bitcast_fusion.2
  86.2 0.4 convolution_bitcast_fusion.3
  86.7 0.9 pad_maximum_fusion.1
  87.6 0.0 all-reduce.2.cloned.1.call-update
  87.6 132.8 %all-reduce.2.cloned.1.call-done = f32[4,384,128]{2,1,0:T(8,128)} async-done(((f32[4,384,128]{2,1,0:T(8,128)}), f32[4,384,128]{2,1,0:T(8,128)}) %all-reduce.2.cloned.1.call-update) | async-done | bytes 786448 | tf_op jit(solution)/shard_map/psum | solution.py:71
  220.4 2.1 broadcast_multiply_fusion
  (11 shorter events, 0.0 us)
Async XLA Ops:
  6.5 13.5 %copy-start.3 = (s32[960]{0:T(1024)S(1)}, s32[960]{0:T(1024)}, u32[]{:S(2)}) copy-start(s32[960]{0:T(1024)} %param.8) | copy-start | bytes 11524
  6.5 13.5 %copy-start.4 = (bf16[48,128]{1,0:T(8,128)(2,1)S(1)}, bf16[48,128]{1,0:T(8,128)(2,1)}, u32[]{:S(2)}) copy-start(bf16[48,128]{1,0:T(8,128)(2,1)} %param.9) | copy-start | bytes 36868
  6.5 38.0 %copy-start.2 = (f32[960]{0:T(1024)S(1)}, f32[960]{0:T(1024)}, u32[]{:S(2)}) copy-start(f32[960]{0:T(1024)} %param.6) | copy-start | bytes 11524
  6.5 38.0 %copy-start.1 = (f32[960]{0:T(1024)S(1)}, f32[960]{0:T(1024)}, u32[]{:S(2)}) copy-start(f32[960]{0:T(1024)} %param.7) | copy-start | bytes 11524
  6.5 213.8 %all-reduce.2.cloned.1.call-start = ((), (), s32[]{:S(2)}) async-start(), calls=%async_computation | async-start | bytes 1572864 | tf_op jit(solution)/shard_map/psum | solution.py:71
  6.6 38.0 %copy-start = (bf16[4,960,384]{2,1,0:T(8,128)(2,1)S(1)}, bf16[4,960,384]{2,1,0:T(8,128)(2,1)}, u32[]{:S(2)}) copy-start(bf16[4,960,384]{2,1,0:T(8,128)(2,1)} %param.5) | copy-start | bytes 8847364
  14.2 31.3 %collective-permute-start = (bf16[4,32,384]{2,0,1:T(4,128)(2,1)S(1)}, bf16[4,32,384]{2,0,1:T(4,128)(2,1)S(1)}, u32[]{:S(2)}, u32[]{:S(2)}) collective-permute-start(bf16[4,32,384]{2,0,1:T(4,128)(2,1)S(1)} %get-tuple-element.10), channel_id=1, source_target_pairs={{0,1},{1,2},{2,3},{3,4},{4,5},{5,6},{6,7},{7,8},{8,9},{9,10},{10,1... | collective-permute-start | bytes 294920 | tf_op jit(solution)/shard_map/ppermute | solution.py:17
  16.3 29.2 %collective-permute-start.1 = (bf16[4,32,384]{2,0,1:T(4,128)(2,1)S(1)}, bf16[4,32,384]{2,0,1:T(4,128)(2,1)S(1)}, u32[]{:S(2)}, u32[]{:S(2)}) collective-permute-start(bf16[4,32,384]{2,0,1:T(4,128)(2,1)S(1)} %get-tuple-element.11), channel_id=1, source_target_pairs={{1,0},{2,1},{3,2},{4,3},{5,4},{6,5},{7,6},{8,7},{9,8},{10,9},{11,1... | collective-permute-start | bytes 294920 | tf_op jit(solution)/shard_map/ppermute | solution.py:20
  49.2 16.9 %slice-start = ((s8[5898240]{0:T(1024)(128)(4,1)}), s8[1703936]{0:T(1024)(128)(4,1)S(1)}, s32[]{:S(2)}) async-start(s8[5898240]{0:T(1024)(128)(4,1)} %bitcast.28), calls=%async_computation.1 | async-start | bytes 3407872
  61.1 5.0 %slice-start.1 = ((s8[5898240]{0:T(1024)(128)(4,1)}), s8[4194304]{0:T(1024)(128)(4,1)S(1)}, s32[]{:S(2)}) async-start(s8[5898240]{0:T(1024)(128)(4,1)} %bitcast.28), calls=%async_computation.2 | async-start | bytes 8388608
Sparse Core Ops, SparseCore 0:
  87.7 132.6 all-reduce.1
where the time goes:
time: 231 us; the launch traced here: 229 us
  waiting for transfers between devices  133 us (58%)
  other arithmetic  34.8 us (15%)
  blocking collectives  24.5 us (11%)
  local copies, waits for them, and re-layouts  15.3 us (7%)
  between operations  13.6 us (6%)
  starting transfers between devices  5.82 us (3%)
  matrix products  2.58 us (1%)
    psum x1, waiting for transfers between devices, on_device(): summed = lax.psum(partial_sum, ('sector', 'tile'))  133 us
    all_gather x1, blocking collectives, on_device(): full_rotation = lax.all_gather(rotation, 'tile', axis=0, tiled=True)  24.5 us
    slice x1, other arithmetic, on_device(): weighted[component]  12 us
    gather x1, local copies, waits for them, and re-layouts, on_device(): neighbors = jnp.take(padded, neighbor_rows, axis=1).astype(jnp.float32)  11.9 us
    unnamed x2, other arithmetic  7.54 us
    convert_element_type x1, other arithmetic, on_device(): neighbors = jnp.take(padded, neighbor_rows, axis=1).astype(jnp.float32)  4.97 us
  transfers between devices with their start and end apart: 3, of which 1 were waited for; matrix products, arithmetic and copies ran while one was open for 0% of the time, Pallas kernels for 0%

commit v1 on v0

v1 whole, which is shorter than its diff:
```python
import functools
import math

import jax
import jax.numpy as jnp
from jax import lax
from jax.experimental import pallas as pl
from jax.experimental.pallas import tpu as pltpu
from jax.sharding import PartitionSpec as P

HALO = 32
GROUP = 8
BLOCK = 192
CHUNK = 128
MESH = pl.DeviceIdType.MESH


def remote(src, dst, send_sem, recv_sem, device):
    return pltpu.make_async_remote_copy(
        src_ref=src,
        dst_ref=dst,
        send_sem=send_sem,
        recv_sem=recv_sem,
        device_id=device,
        device_id_type=MESH,
    )


def kernel(
    sectors, tiles, gather_rotation,
    snap_ref, dens_ref, speed_ref, off_ref, rot_ref,
    out_ref,
    pad, rows, weighted, fields, rot_all, part, core_in, x_out, x_in, own, slots, far,
    load_sem, halo_send, halo_recv, rot_send, rot_recv, core_send, core_recv, x_send, x_recv,
    rs_send, rs_recv, far_send, far_recv, ag_send, ag_recv, agx_send, agx_recv, agc_send, agc_recv,
):
    comps, cells, snaps = snap_ref.shape
    chunks = snaps // CHUNK
    share = CHUNK // GROUP
    groups = tiles // GROUP
    cell_total = cells * sectors * tiles

    s = lax.axis_index("sector")
    t = lax.axis_index("tile")
    core = lax.rem(s, 2)
    side = s // 2
    low = lax.rem(t, GROUP)
    high = t // GROUP
    comp = 2 * core + side
    other_core = (s + 1 - 2 * core, t)
    other_side = (lax.rem(s + 2, sectors), t)

    def group_tile(step):
        return high * GROUP + lax.rem(low + step, GROUP)

    def far_tile(step):
        return lax.rem(high + step, groups) * GROUP + low

    me = s * tiles + t
    total = sectors * tiles
    right_index = lax.rem(me + 1, total)
    left_index = lax.rem(me + total - 1, total)
    right = (right_index // tiles, lax.rem(right_index, tiles))
    left = (left_index // tiles, lax.rem(left_index, tiles))

    loads = [
        pltpu.make_async_copy(
            snap_ref.at[c], pad.at[c, pl.ds(HALO, cells)], load_sem.at[c]
        )
        for c in range(comps)
    ]
    for load in loads:
        load.start()

    peers = [left, right, other_core, other_side]
    peers += [(s, group_tile(d)) for d in range(1, GROUP)]
    peers += [(s, far_tile(e)) for e in range(1, groups)]
    barrier = pltpu.get_barrier_semaphore()
    for peer in peers:
        pl.semaphore_signal(barrier, inc=1, device_id=peer, device_id_type=MESH)

    rows[...] = jnp.zeros_like(rows)
    dens = dens_ref[...]
    speed = speed_ref[...]
    rows[0:1, 0:cells] = dens
    rows[1:2, 0:cells] = 1.0 / (dens * speed * speed)
    rows[2:3, 0:cells] = 0.5 / speed
    rows[3:4, 0:cells] = off_ref[...].astype(jnp.float32) + HALO
    columns = rows[...].T

    pl.semaphore_wait(barrier, len(peers))
    sends = []
    depth = rot_ref.shape[0]
    if gather_rotation:
        def rot_at(tile):
            return pl.ds(pl.multiple_of(tile * depth, 16), depth)

        for d in range(1, tiles):
            copy = remote(
                rot_ref, rot_all.at[rot_at(t)], rot_send.at[d], rot_recv.at[d],
                (s, lax.rem(t + d, tiles)),
            )
            copy.start()
            sends.append(copy)
        rot_all[rot_at(t), :] = rot_ref[...]
    else:
        rot_all[...] = rot_ref[...]
    to_right = remote(
        snap_ref.at[:, pl.ds(cells - HALO, HALO)], pad.at[:, pl.ds(0, HALO)],
        halo_send.at[0], halo_recv.at[0], right,
    )
    to_left = remote(
        snap_ref.at[:, pl.ds(0, HALO)], pad.at[:, pl.ds(HALO + cells, HALO)],
        halo_send.at[1], halo_recv.at[1], left,
    )
    to_right.start()
    to_left.start()
    sends += [to_right, to_left]

    window = BLOCK + 2 * HALO
    shift = (
        lax.broadcasted_iota(jnp.int32, (BLOCK, window), 1)
        - lax.broadcasted_iota(jnp.int32, (BLOCK, window), 0)
    ).astype(jnp.float32)
    own_cell = jnp.where(shift == HALO, 1.0, 0.0)

    def weigh(block):
        first = block * BLOCK
        column = columns[first : first + BLOCK]
        dens_c, inverse, slope, target = (column[:, i : i + 1] for i in range(4))
        pick = (jnp.where(shift == target, 1.0, 0.0) - own_cell).astype(jnp.bfloat16)

        def change(c):
            return jnp.dot(
                pick, pad[c, first : first + window, :], preferred_element_type=jnp.float32
            )

        def local(c):
            return pad[c, HALO + first : HALO + first + BLOCK, :].astype(jnp.float32)

        d_sum = (change(1) + change(2)) + change(3)
        weighted[0, first : first + BLOCK, :] = (
            local(0) * inverse + d_sum * slope
        ).astype(jnp.bfloat16)
        push = change(0) * slope
        for c in range(1, comps):
            weighted[c, first : first + BLOCK, :] = (dens_c * local(c) + push).astype(
                jnp.bfloat16
            )

    for load in loads:
        load.wait()
    blocks = cells // BLOCK
    for block in range(1, blocks - 1):
        weigh(block)

    if gather_rotation:
        for d in range(1, tiles):
            source = lax.rem(t + tiles - d, tiles)
            remote(
                rot_ref, rot_all.at[rot_at(source)], rot_send.at[d], rot_recv.at[d],
                (s, source),
            ).wait_recv()
    for c in range(comps):
        fields[c] = jnp.dot(
            pad[c, HALO : HALO + cells, :], rot_all[...], preferred_element_type=jnp.float32
        ).astype(jnp.bfloat16)

    to_right.wait_recv()
    to_left.wait_recv()
    weigh(0)
    weigh(blocks - 1)

    def span(q):
        return pl.ds(q * CHUNK, CHUNK)

    def shard(q, lo):
        return pl.ds(pl.multiple_of(q * CHUNK + lo * share, share), share)

    def core_copy(q):
        return remote(
            part.at[pl.ds(2 * (1 - core), 2), span(q)], core_in.at[q],
            core_send.at[q], core_recv.at[q], other_core,
        )

    def x_copy(q):
        return remote(x_out.at[q], x_in.at[q], x_send.at[q], x_recv.at[q], other_side)

    def rs_copy(q, d):
        lo = lax.rem(low + d, GROUP)
        return remote(
            own.at[q, pl.ds(pl.multiple_of(lo * share, share), share)], slots.at[q, d],
            rs_send.at[q, d], rs_recv.at[q, d], (s, group_tile(d)),
        )

    def far_copy(q, e):
        return remote(
            far.at[q, high], far.at[q, high],
            far_send.at[q, e], far_recv.at[q, e], (s, far_tile(e)),
        )

    def ag_copy(q, d):
        place = out_ref.at[comp, shard(q, low)]
        return remote(place, place, ag_send.at[q, d], ag_recv.at[q, d], (s, group_tile(d)))

    def agx_copy(q):
        place = out_ref.at[comp, span(q)]
        return remote(place, place, agx_send.at[q], agx_recv.at[q], other_side)

    def agc_copy(q):
        place = out_ref.at[pl.ds(2 * core, 2), span(q)]
        return remote(place, place, agc_send.at[q], agc_recv.at[q], other_core)

    def begin(copy):
        copy.start()
        sends.append(copy)

    def project(q):
        for c in range(comps):
            part[c, q * CHUNK : (q + 1) * CHUNK, :] = lax.dot_general(
                weighted[c, :, q * CHUNK : (q + 1) * CHUNK],
                fields[c],
                (((0,), (0,)), ((), ())),
                preferred_element_type=jnp.float32,
            )
        begin(core_copy(q))

    def over_core(q):
        core_copy(q).wait_recv()
        x_out[q] = part[2 * core + 1 - side, q * CHUNK : (q + 1) * CHUNK, :] + core_in[q, 1 - side]
        begin(x_copy(q))
        own[q] = part[comp, q * CHUNK : (q + 1) * CHUNK, :] + core_in[q, side]

    def over_side(q):
        x_copy(q).wait_recv()
        own[q] = own[q] + x_in[q]
        for d in range(1, GROUP):
            begin(rs_copy(q, d))

    def over_tiles(q):
        for d in range(1, GROUP):
            rs_copy(q, d).wait_recv()
        value = own[q, pl.ds(pl.multiple_of(low * share, share), share), :]
        for d in range(1, GROUP):
            value = value + slots[q, d]
        if groups > 1:
            far[q, high] = value
            for e in range(1, groups):
                begin(far_copy(q, e))
            for e in range(1, groups):
                source = lax.rem(high + groups - e, groups)
                remote(
                    far.at[q, source], far.at[q, source],
                    far_send.at[q, e], far_recv.at[q, e], (s, far_tile(e)),
                ).wait_recv()
            value = far[q, 0]
            for e in range(1, groups):
                value = value + far[q, e]
        out_ref[comp, shard(q, low), :] = value / math.sqrt(cell_total)
        for d in range(1, GROUP):
            begin(ag_copy(q, d))

    def back_side(q):
        for d in range(1, GROUP):
            place = out_ref.at[comp, shard(q, lax.rem(low + GROUP - d, GROUP))]
            remote(
                place, place, ag_send.at[q, d], ag_recv.at[q, d], (s, group_tile(d))
            ).wait_recv()
        begin(agx_copy(q))

    def back_core(q):
        place = out_ref.at[2 * core + 1 - side, span(q)]
        remote(place, place, agx_send.at[q], agx_recv.at[q], other_side).wait_recv()
        begin(agc_copy(q))

    def finish(q):
        place = out_ref.at[pl.ds(2 * (1 - core), 2), span(q)]
        remote(place, place, agc_send.at[q], agc_recv.at[q], other_core).wait_recv()

    stages = [project, over_core, over_side, over_tiles, back_side, back_core, finish]
    for step in range(chunks + len(stages) - 1):
        for index, stage in enumerate(stages):
            if 0 <= step - index < chunks:
                stage(step - index)
    for copy in sends:
        copy.wait_send()


def on_device(sectors, tiles, snapshots, density, sound_speed, offsets, rotation):
    comps, cells, snaps = snapshots.shape
    gather_rotation = rotation.shape[0] % 16 == 0
    if not gather_rotation:
        rotation = lax.all_gather(rotation, "tile", axis=0, tiled=True)
    modes = rotation.shape[1]
    chunks = snaps // CHUNK
    share = CHUNK // GROUP
    groups = tiles // GROUP
    wide = -(-cells // 128) * 128
    f32, bf16 = jnp.float32, jnp.bfloat16
    dma = pltpu.SemaphoreType.DMA
    vmem = pl.BlockSpec(memory_space=pltpu.VMEM)
    return pl.pallas_call(
        functools.partial(kernel, sectors, tiles, gather_rotation),
        out_shape=jax.ShapeDtypeStruct((comps, snaps, modes), f32),
        in_specs=[pl.BlockSpec(memory_space=pl.ANY), vmem, vmem, vmem, vmem],
        out_specs=vmem,
        scratch_shapes=[
            pltpu.VMEM((comps, cells + 2 * HALO, snaps), bf16),
            pltpu.VMEM((8, wide), f32),
            pltpu.VMEM((comps, cells, snaps), bf16),
            pltpu.VMEM((comps, cells, modes), bf16),
            pltpu.VMEM((snaps, modes), bf16),
            pltpu.VMEM((comps, snaps, modes), f32),
            pltpu.VMEM((chunks, 2, CHUNK, modes), f32),
            pltpu.VMEM((chunks, CHUNK, modes), f32),
            pltpu.VMEM((chunks, CHUNK, modes), f32),
            pltpu.VMEM((chunks, CHUNK, modes), f32),
            pltpu.VMEM((chunks, GROUP, share, modes), f32),
            pltpu.VMEM((chunks, groups, share, modes), f32),
            dma((comps,)),
            dma((2,)),
            dma((2,)),
            dma((tiles,)),
            dma((tiles,)),
            dma((chunks,)),
            dma((chunks,)),
            dma((chunks,)),
            dma((chunks,)),
            dma((chunks, GROUP)),
            dma((chunks, GROUP)),
            dma((chunks, groups)),
            dma((chunks, groups)),
            dma((chunks, GROUP)),
            dma((chunks, GROUP)),
            dma((chunks,)),
            dma((chunks,)),
            dma((chunks,)),
            dma((chunks,)),
        ],
        compiler_params=pltpu.CompilerParams(
            collective_id=0, has_side_effects=True, vmem_limit_bytes=40 * 1024 * 1024
        ),
        cost_estimate=pl.CostEstimate(
            flops=4 * cells * comps * snaps * modes, bytes_accessed=2 * comps * cells * snaps,
            transcendentals=0,
        ),
    )(snapshots, density[None], sound_speed[None], offsets[None], rotation)


def solution(mesh):
    sectors, tiles = mesh.shape["sector"], mesh.shape["tile"]
    return jax.shard_map(
        functools.partial(on_device, sectors, tiles),
        mesh=mesh,
        in_specs=(
            P(None, ("sector", "tile"), None),
            P(("sector", "tile")),
            P(("sector", "tile")),
            P(("sector", "tile")),
            P("tile", None),
        ),
        out_specs=P(),
        check_vma=False,
    )
```

time: 231 us -> 45 us (0.19)
  waiting for transfers between devices: 133 us -> 0 us
  Pallas kernels: 0 us -> 39.2 us
  other arithmetic: 34.8 us -> 0 us
  blocking collectives: 24.5 us -> 0 us
  between operations: 13.6 us -> 0.01 us
  local copies, waits for them, and re-layouts: 15.3 us -> 5.48 us
  starting transfers between devices: 5.82 us -> 0 us
  matrix products: 2.58 us -> 0 us
    psum x1 -> x0, waiting for transfers between devices: 133 us -> none  [on_device(): summed = lax.psum(partial_sum, ('sector', 'tile'))]
    pallas_call x0 -> x1, Pallas kernels: none -> 39.2 us  [on_device(): pl.pallas_call(functools.partial(kernel, sectors, tiles, gather_rotation)...]
    all_gather x1 -> x0, blocking collectives: 24.5 us -> none  [on_device(): full_rotation = lax.all_gather(rotation, 'tile', axis=0, tiled=True)]
    slice x1 -> x0, other arithmetic: 12 us -> none  [on_device(): weighted[component]]
    gather x1 -> x0, local copies, waits for them, and re-layouts: 11.9 us -> none  [on_device(): neighbors = jnp.take(padded, neighbor_rows, axis=1).astype(jnp.float32)]
    unnamed x2 -> x0, other arithmetic: 7.54 us -> none
    ppermute x2 -> x0, starting transfers between devices: 5.79 us -> none  [the longest x1 3.66 us: padded_2(): lax.ppermute(lax.slice_in_dim(block, 0, width, axis=dim), axis, backward)]
    unnamed x15 -> x11, local copies, waits for them, and re-layouts: 0.12 us -> 5.48 us
  transfers between devices with their start and end apart: 3 -> 0, of which waited for: 1 -> 0; matrix products, arithmetic and copies ran while one was open for 0% -> 0% of each run, Pallas kernels for 0% -> 0%
where the time goes in v1:
time: 45 us; the launch traced here: 44.7 us
  Pallas kernels  39.2 us (87%)
  local copies, waits for them, and re-layouts  5.48 us (12%)
    pallas_call x1, Pallas kernels, on_device(): pl.pallas_call(functools.partial(kernel, sectors, tiles, gather_rotation)...  39.2 us
    unnamed x11, local copies, waits for them, and re-layouts  5.48 us

profile of v1, /device:TPU:1, one launch (start us, length us, event | category | flops | bytes accessed | tf_op | source)
XLA Modules:
  0.0 44.7 jit_solution(7943554200865040782)
XLA Ops:
  0.0 0.0 copy-start
  0.0 1.8 %copy-done = bf16[4,960,384]{2,1,0:T(8,128)(2,1)S(1)} copy-done((bf16[4,960,384]{2,1,0:T(8,128)(2,1)S(1)}, bf16[4,960,384]{2,1,0:T(8,128)(2,1)}, u32[]{:S(2)}) %copy-start) | copy-done | bytes 2949144
  1.8 0.0 copy-start.1
  1.8 0.7 %copy-done.1 = bf16[48,128]{1,0:T(8,128)(2,1)S(1)} copy-done((bf16[48,128]{1,0:T(8,128)(2,1)S(1)}, bf16[48,128]{1,0:T(8,128)(2,1)}, u32[]{:S(2)}) %copy-start.1) | copy-done | bytes 12312
  2.5 0.0 copy-start.2
  2.5 0.7 %copy-done.2 = f32[960]{0:T(1024)S(1)} copy-done((f32[960]{0:T(1024)S(1)}, f32[960]{0:T(1024)}, u32[]{:S(2)}) %copy-start.2) | copy-done | bytes 3864
  3.2 0.0 copy-start.3
  3.2 0.7 %copy-done.3 = f32[960]{0:T(1024)S(1)} copy-done((f32[960]{0:T(1024)S(1)}, f32[960]{0:T(1024)}, u32[]{:S(2)}) %copy-start.3) | copy-done | bytes 3864
  3.9 0.0 copy-start.4
  3.9 0.7 %copy-done.4 = s32[960]{0:T(1024)S(1)} copy-done((s32[960]{0:T(1024)S(1)}, s32[960]{0:T(1024)}, u32[]{:S(2)}) %copy-start.4) | copy-done | bytes 3864
  4.6 39.2 %shard_map.55 = f32[4,384,128]{2,1,0:T(8,128)S(1)} custom-call(bf16[4,960,384]{2,1,0:T(8,128)(2,1)S(1)} %copy-done, f32[1,960]{1,0:T(1,128)S(1)} %bitcast.3, f32[1,960]{1,0:T(1,128)S(1)} %bitcast.4, s32[1,960]{1,0:T(1,128)S(1)} %bitcast.5, bf16[48,128]{1,0:T(8,128)(2,1)S(1)} %copy-done.1), custom_call_target="tpu_custom_call" | custom-call | flops 754974720 | bytes 2949120 | tf_op jit(solution)/shard_map/pallas_call | solution.py:302
  43.8 0.9 %copy.7 = f32[4,384,128]{2,1,0:T(8,128)} copy(f32[4,384,128]{2,1,0:T(8,128)S(1)} %shard_map.55) | data formatting | bytes 1572864
Async XLA Ops:
  0.0 1.8 %copy-start = (bf16[4,960,384]{2,1,0:T(8,128)(2,1)S(1)}, bf16[4,960,384]{2,1,0:T(8,128)(2,1)}, u32[]{:S(2)}) copy-start(bf16[4,960,384]{2,1,0:T(8,128)(2,1)} %snap_ref.1) | copy-start | bytes 8847364
  1.8 0.7 %copy-start.1 = (bf16[48,128]{1,0:T(8,128)(2,1)S(1)}, bf16[48,128]{1,0:T(8,128)(2,1)}, u32[]{:S(2)}) copy-start(bf16[48,128]{1,0:T(8,128)(2,1)} %rot_ref.1) | copy-start | bytes 36868
  2.5 0.7 %copy-start.2 = (f32[960]{0:T(1024)S(1)}, f32[960]{0:T(1024)}, u32[]{:S(2)}) copy-start(f32[960]{0:T(1024)} %param.6) | copy-start | bytes 11524
  3.2 0.7 %copy-start.3 = (f32[960]{0:T(1024)S(1)}, f32[960]{0:T(1024)}, u32[]{:S(2)}) copy-start(f32[960]{0:T(1024)} %param.7) | copy-start | bytes 11524
  3.9 0.7 %copy-start.4 = (s32[960]{0:T(1024)S(1)}, s32[960]{0:T(1024)}, u32[]{:S(2)}) copy-start(s32[960]{0:T(1024)} %param.8) | copy-start | bytes 11524

commit v2 on v1

--- a/solution.py
+++ b/solution.py
@@ -12,6 +12,7 @@
 GROUP = 8
 BLOCK = 192
 CHUNK = 128
+SPACING = 1.5
 MESH = pl.DeviceIdType.MESH
 
 
@@ -30,8 +31,8 @@
     sectors, tiles, gather_rotation,
     snap_ref, dens_ref, speed_ref, off_ref, rot_ref,
     out_ref,
-    pad, rows, weighted, fields, rot_all, part, core_in, x_out, x_in, own, slots, far,
-    load_sem, halo_send, halo_recv, rot_send, rot_recv, core_send, core_recv, x_send, x_recv,
+    dens_in, speed_in, off_in, pad, rows, weighted, fields, rot_all, part, core_in, x_out, x_in, own, slots, far,
+    load_sem, cell_sem, own_rot_sem, halo_send, halo_recv, rot_send, rot_recv, core_send, core_recv, x_send, x_recv,
     rs_send, rs_recv, far_send, far_recv, ag_send, ag_recv, agx_send, agx_recv, agc_send, agc_recv,
 ):
     comps, cells, snaps = snap_ref.shape
@@ -69,7 +70,13 @@
         )
         for c in range(comps)
     ]
-    for load in loads:
+    cell_loads = [
+        pltpu.make_async_copy(source, target, cell_sem.at[i])
+        for i, (source, target) in enumerate(
+            ((dens_ref, dens_in), (speed_ref, speed_in), (off_ref, off_in))
+        )
+    ]
+    for load in cell_loads + loads:
         load.start()
 
     peers = [left, right, other_core, other_side]
@@ -80,12 +87,14 @@
         pl.semaphore_signal(barrier, inc=1, device_id=peer, device_id_type=MESH)
 
     rows[...] = jnp.zeros_like(rows)
-    dens = dens_ref[...]
-    speed = speed_ref[...]
+    for load in cell_loads:
+        load.wait()
+    dens = dens_in[...]
+    speed = speed_in[...]
     rows[0:1, 0:cells] = dens
     rows[1:2, 0:cells] = 1.0 / (dens * speed * speed)
     rows[2:3, 0:cells] = 0.5 / speed
-    rows[3:4, 0:cells] = off_ref[...].astype(jnp.float32) + HALO
+    rows[3:4, 0:cells] = off_in[...].astype(jnp.float32) + HALO
     columns = rows[...].T
 
     pl.semaphore_wait(barrier, len(peers))
@@ -102,9 +111,10 @@
             )
             copy.start()
             sends.append(copy)
-        rot_all[rot_at(t), :] = rot_ref[...]
+        own_rot = pltpu.make_async_copy(rot_ref, rot_all.at[rot_at(t)], own_rot_sem.at[0])
     else:
-        rot_all[...] = rot_ref[...]
+        own_rot = pltpu.make_async_copy(rot_ref, rot_all, own_rot_sem.at[0])
+    own_rot.start()
     to_right = remote(
         snap_ref.at[:, pl.ds(cells - HALO, HALO)], pad.at[:, pl.ds(0, HALO)],
         halo_send.at[0], halo_recv.at[0], right,
@@ -124,27 +134,28 @@
     ).astype(jnp.float32)
     own_cell = jnp.where(shift == HALO, 1.0, 0.0)
 
-    def weigh(block):
+    def weigh(block, q):
         first = block * BLOCK
+        lanes = slice(q * CHUNK, (q + 1) * CHUNK)
         column = columns[first : first + BLOCK]
         dens_c, inverse, slope, target = (column[:, i : i + 1] for i in range(4))
         pick = (jnp.where(shift == target, 1.0, 0.0) - own_cell).astype(jnp.bfloat16)
 
         def change(c):
             return jnp.dot(
-                pick, pad[c, first : first + window, :], preferred_element_type=jnp.float32
+                pick, pad[c, first : first + window, lanes], preferred_element_type=jnp.float32
             )
 
         def local(c):
-            return pad[c, HALO + first : HALO + first + BLOCK, :].astype(jnp.float32)
+            return pad[c, HALO + first : HALO + first + BLOCK, lanes].astype(jnp.float32)
 
         d_sum = (change(1) + change(2)) + change(3)
-        weighted[0, first : first + BLOCK, :] = (
+        weighted[0, first : first + BLOCK, lanes] = (
             local(0) * inverse + d_sum * slope
         ).astype(jnp.bfloat16)
         push = change(0) * slope
         for c in range(1, comps):
-            weighted[c, first : first + BLOCK, :] = (dens_c * local(c) + push).astype(
+            weighted[c, first : first + BLOCK, lanes] = (dens_c * local(c) + push).astype(
                 jnp.bfloat16
             )
 
@@ -152,7 +163,7 @@
         load.wait()
     blocks = cells // BLOCK
     for block in range(1, blocks - 1):
-        weigh(block)
+        weigh(block, 0)
 
     if gather_rotation:
         for d in range(1, tiles):
@@ -161,6 +172,7 @@
                 rot_ref, rot_all.at[rot_at(source)], rot_send.at[d], rot_recv.at[d],
                 (s, source),
             ).wait_recv()
+    own_rot.wait()
     for c in range(comps):
         fields[c] = jnp.dot(
             pad[c, HALO : HALO + cells, :], rot_all[...], preferred_element_type=jnp.float32
@@ -168,8 +180,8 @@
 
     to_right.wait_recv()
     to_left.wait_recv()
-    weigh(0)
-    weigh(blocks - 1)
+    weigh(0, 0)
+    weigh(blocks - 1, 0)
 
     def span(q):
         return pl.ds(q * CHUNK, CHUNK)
@@ -216,6 +228,9 @@
         sends.append(copy)
 
     def project(q):
+        if q > 0:
+            for block in range(blocks):
+                weigh(block, q)
         for c in range(comps):
             part[c, q * CHUNK : (q + 1) * CHUNK, :] = lax.dot_general(
                 weighted[c, :, q * CHUNK : (q + 1) * CHUNK],
@@ -278,10 +293,13 @@
         remote(place, place, agc_send.at[q], agc_recv.at[q], other_core).wait_recv()
 
     stages = [project, over_core, over_side, over_tiles, back_side, back_core, finish]
-    for step in range(chunks + len(stages) - 1):
-        for index, stage in enumerate(stages):
-            if 0 <= step - index < chunks:
-                stage(step - index)
+    expected = (0.0, 1.2, 3.5, 6.8, 10.1, 12.4, 13.6)
+    for _, q, index in sorted(
+        (SPACING * q + expected[index], q, index)
+        for q in range(chunks)
+        for index in range(len(stages))
+    ):
+        stages[index](q)
     for copy in sends:
         copy.wait_send()
 
@@ -299,12 +317,16 @@
     f32, bf16 = jnp.float32, jnp.bfloat16
     dma = pltpu.SemaphoreType.DMA
     vmem = pl.BlockSpec(memory_space=pltpu.VMEM)
+    hbm = pl.BlockSpec(memory_space=pltpu.HBM)
     return pl.pallas_call(
         functools.partial(kernel, sectors, tiles, gather_rotation),
         out_shape=jax.ShapeDtypeStruct((comps, snaps, modes), f32),
-        in_specs=[pl.BlockSpec(memory_space=pl.ANY), vmem, vmem, vmem, vmem],
+        in_specs=[hbm] * 5,
         out_specs=vmem,
         scratch_shapes=[
+            pltpu.VMEM((1, cells), f32),
+            pltpu.VMEM((1, cells), f32),
+            pltpu.VMEM((1, cells), jnp.int32),
             pltpu.VMEM((comps, cells + 2 * HALO, snaps), bf16),
             pltpu.VMEM((8, wide), f32),
             pltpu.VMEM((comps, cells, snaps), bf16),
@@ -318,6 +340,8 @@
             pltpu.VMEM((chunks, GROUP, share, modes), f32),
             pltpu.VMEM((chunks, groups, share, modes), f32),
             dma((comps,)),
+            dma((3,)),
+            dma((1,)),
             dma((2,)),
             dma((2,)),
             dma((tiles,)),
@@ -338,7 +362,7 @@
             dma((chunks,)),
         ],
         compiler_params=pltpu.CompilerParams(
-            collective_id=0, has_side_effects=True, vmem_limit_bytes=40 * 1024 * 1024
+            collective_id=0, has_side_effects=True, vmem_limit_bytes=64 * 1024 * 1024
         ),
         cost_estimate=pl.CostEstimate(
             flops=4 * cells * comps * snaps * modes, bytes_accessed=2 * comps * cells * snaps,

time: 45 us -> 40.7 us (0.904)
  local copies, waits for them, and re-layouts: 5.48 us -> 2.06 us
  Pallas kernels: 39.2 us -> 38.5 us
    unnamed x11 -> x1, local copies, waits for them, and re-layouts: 5.48 us -> 2.06 us
    pallas_call x1, Pallas kernels: 39.2 us -> 38.5 us  [on_device(): pl.pallas_call(functools.partial(kernel, sectors, tiles, gather_rotation)...]
where the time goes in v2:
time: 40.7 us; the launch traced here: 40.5 us
  Pallas kernels  38.5 us (95%)
  local copies, waits for them, and re-layouts  2.06 us (5%)
    pallas_call x1, Pallas kernels, on_device(): pl.pallas_call(functools.partial(kernel, sectors, tiles, gather_rotation)...  38.5 us
    unnamed x1, local copies, waits for them, and re-layouts  2.06 us

profile of v2, /device:TPU:1, one launch (start us, length us, event | category | flops | bytes accessed | tf_op | source)
XLA Modules:
  0.0 40.5 jit_solution(6068109880437965264)
XLA Ops:
  0.0 38.5 %shard_map.55 = f32[4,384,128]{2,1,0:T(8,128)} custom-call(bf16[4,960,384]{2,1,0:T(8,128)(2,1)} %snap_ref.1, f32[1,960]{1,0:T(1,128)} %bitcast.3, f32[1,960]{1,0:T(1,128)} %bitcast.4, s32[1,960]{1,0:T(1,128)} %bitcast.5, bf16[48,128]{1,0:T(8,128)(2,1)} %rot_ref.1), custom_call_target="tpu_custom_call" | custom-call | flops 754974720 | bytes 2949120 | tf_op jit(solution)/shard_map/pallas_call | solution.py:321
  38.5 2.1 %copy.7 = f32[4,384,128]{2,1,0:T(8,128)} copy(f32[4,384,128]{2,1,0:T(8,128)} %shard_map.55) | data formatting | bytes 1572864

commit v3 on v2

--- a/solution.py
+++ b/solution.py
@@ -31,7 +31,7 @@
     sectors, tiles, gather_rotation,
     snap_ref, dens_ref, speed_ref, off_ref, rot_ref,
     out_ref,
-    dens_in, speed_in, off_in, pad, rows, weighted, fields, rot_all, part, core_in, x_out, x_in, own, slots, far,
+    dens_in, speed_in, off_in, pad, rows, columns, weighted, fields, rot_all, part, core_in, x_out, x_in, own, slots, far,
     load_sem, cell_sem, own_rot_sem, halo_send, halo_recv, rot_send, rot_recv, core_send, core_recv, x_send, x_recv,
     rs_send, rs_recv, far_send, far_recv, ag_send, ag_recv, agx_send, agx_recv, agc_send, agc_recv,
 ):
@@ -39,7 +39,6 @@
     chunks = snaps // CHUNK
     share = CHUNK // GROUP
     groups = tiles // GROUP
-    cell_total = cells * sectors * tiles
 
     s = lax.axis_index("sector")
     t = lax.axis_index("tile")
@@ -95,7 +94,7 @@
     rows[1:2, 0:cells] = 1.0 / (dens * speed * speed)
     rows[2:3, 0:cells] = 0.5 / speed
     rows[3:4, 0:cells] = off_in[...].astype(jnp.float32) + HALO
-    columns = rows[...].T
+    columns[...] = rows[...].T
 
     pl.semaphore_wait(barrier, len(peers))
     sends = []
@@ -134,36 +133,35 @@
     ).astype(jnp.float32)
     own_cell = jnp.where(shift == HALO, 1.0, 0.0)
 
-    def weigh(block, q):
-        first = block * BLOCK
-        lanes = slice(q * CHUNK, (q + 1) * CHUNK)
-        column = columns[first : first + BLOCK]
+    def weigh(block):
+        first = pl.multiple_of(block * BLOCK, 16)
+        own_rows = pl.ds(first, BLOCK)
+        center = pl.ds(pl.multiple_of(first + HALO, 16), BLOCK)
+        column = columns[own_rows, :]
         dens_c, inverse, slope, target = (column[:, i : i + 1] for i in range(4))
         pick = (jnp.where(shift == target, 1.0, 0.0) - own_cell).astype(jnp.bfloat16)
 
         def change(c):
             return jnp.dot(
-                pick, pad[c, first : first + window, lanes], preferred_element_type=jnp.float32
+                pick, pad[c, pl.ds(first, window), :], preferred_element_type=jnp.float32
             )
 
         def local(c):
-            return pad[c, HALO + first : HALO + first + BLOCK, lanes].astype(jnp.float32)
+            return pad[c, center, :].astype(jnp.float32)
 
         d_sum = (change(1) + change(2)) + change(3)
-        weighted[0, first : first + BLOCK, lanes] = (
-            local(0) * inverse + d_sum * slope
-        ).astype(jnp.bfloat16)
+        weighted[0, own_rows, :] = (local(0) * inverse + d_sum * slope).astype(jnp.bfloat16)
         push = change(0) * slope
         for c in range(1, comps):
-            weighted[c, first : first + BLOCK, lanes] = (dens_c * local(c) + push).astype(
-                jnp.bfloat16
-            )
+            weighted[c, own_rows, :] = (dens_c * local(c) + push).astype(jnp.bfloat16)
 
     for load in loads:
         load.wait()
     blocks = cells // BLOCK
-    for block in range(1, blocks - 1):
-        weigh(block, 0)
+
+    @pl.loop(1, blocks - 1)
+    def _(block):
+        weigh(block)
 
     if gather_rotation:
         for d in range(1, tiles):
@@ -173,15 +171,19 @@
                 (s, source),
             ).wait_recv()
     own_rot.wait()
-    for c in range(comps):
+
+    @pl.loop(0, comps)
+    def _(c):
         fields[c] = jnp.dot(
             pad[c, HALO : HALO + cells, :], rot_all[...], preferred_element_type=jnp.float32
         ).astype(jnp.bfloat16)
 
     to_right.wait_recv()
     to_left.wait_recv()
-    weigh(0, 0)
-    weigh(blocks - 1, 0)
+
+    @pl.loop(0, 2)
+    def _(end):
+        weigh(end * (blocks - 1))
 
     def span(q):
         return pl.ds(q * CHUNK, CHUNK)
@@ -228,10 +230,8 @@
         sends.append(copy)
 
     def project(q):
-        if q > 0:
-            for block in range(blocks):
-                weigh(block, q)
-        for c in range(comps):
+        @pl.loop(0, comps)
+        def _(c):
             part[c, q * CHUNK : (q + 1) * CHUNK, :] = lax.dot_general(
                 weighted[c, :, q * CHUNK : (q + 1) * CHUNK],
                 fields[c],
@@ -271,7 +271,7 @@
             value = far[q, 0]
             for e in range(1, groups):
                 value = value + far[q, e]
-        out_ref[comp, shard(q, low), :] = value / math.sqrt(cell_total)
+        out_ref[comp, shard(q, low), :] = value
         for d in range(1, GROUP):
             begin(ag_copy(q, d))
 
@@ -318,7 +318,7 @@
     dma = pltpu.SemaphoreType.DMA
     vmem = pl.BlockSpec(memory_space=pltpu.VMEM)
     hbm = pl.BlockSpec(memory_space=pltpu.HBM)
-    return pl.pallas_call(
+    summed = pl.pallas_call(
         functools.partial(kernel, sectors, tiles, gather_rotation),
         out_shape=jax.ShapeDtypeStruct((comps, snaps, modes), f32),
         in_specs=[hbm] * 5,
@@ -329,6 +329,7 @@
             pltpu.VMEM((1, cells), jnp.int32),
             pltpu.VMEM((comps, cells + 2 * HALO, snaps), bf16),
             pltpu.VMEM((8, wide), f32),
+            pltpu.VMEM((wide, 8), f32),
             pltpu.VMEM((comps, cells, snaps), bf16),
             pltpu.VMEM((comps, cells, modes), bf16),
             pltpu.VMEM((snaps, modes), bf16),
@@ -369,6 +370,7 @@
             transcendentals=0,
         ),
     )(snapshots, density[None], sound_speed[None], offsets[None], rotation)
+    return summed / math.sqrt(cells * sectors * tiles)
 
 
 def solution(mesh):

time: 40.7 us -> 41.8 us (1.027)
  other arithmetic: 0 us -> 2.08 us
  local copies, waits for them, and re-layouts: 2.06 us -> 0 us
  Pallas kernels: 38.5 us -> 39.6 us
    div x0 -> x1, other arithmetic: none -> 2.08 us  [on_device(): return summed / math.sqrt(cells * sectors * tiles)]
    unnamed x1 -> x0, local copies, waits for them, and re-layouts: 2.06 us -> none
    pallas_call x1, Pallas kernels: 38.5 us -> 39.6 us  [on_device(): pl.pallas_call(functools.partial(kernel, sectors, tiles, gather_rotation)...]
where the time goes in v3:
time: 41.8 us; the launch traced here: 41.7 us
  Pallas kernels  39.6 us (95%)
  other arithmetic  2.08 us (5%)
    pallas_call x1, Pallas kernels, on_device(): pl.pallas_call(functools.partial(kernel, sectors, tiles, gather_rotation)...  39.6 us
    div x1, other arithmetic, on_device(): return summed / math.sqrt(cells * sectors * tiles)  2.08 us

profile of v3, /device:TPU:1, one launch (start us, length us, event | category | flops | bytes accessed | tf_op | source)
XLA Modules:
  0.0 41.7 jit_solution(6557316621915238168)
XLA Ops:
  0.0 39.6 %shard_map.55 = f32[4,384,128]{2,1,0:T(8,128)} custom-call(bf16[4,960,384]{2,1,0:T(8,128)(2,1)} %snap_ref.1, f32[1,960]{1,0:T(1,128)} %bitcast.3, f32[1,960]{1,0:T(1,128)} %bitcast.4, s32[1,960]{1,0:T(1,128)} %bitcast.5, bf16[48,128]{1,0:T(8,128)(2,1)} %rot_ref.1), custom_call_target="tpu_custom_call" | custom-call | flops 754974720 | bytes 2949120 | tf_op jit(solution)/shard_map/pallas_call | solution.py:321
  39.6 2.1 %broadcast_multiply_fusion = f32[4,384,128]{2,1,0:T(8,128)} fusion(f32[4,384,128]{2,1,0:T(8,128)} %shard_map.55), kind=kLoop, calls=%fused_computation | loop fusion | flops 196608 | bytes 1572864 | tf_op jit(solution)/shard_map/div | solution.py:373

commit v4 on v2

--- a/solution.py
+++ b/solution.py
@@ -10,6 +10,7 @@
 
 HALO = 32
 GROUP = 8
+DEEP = 4
 BLOCK = 192
 CHUNK = 128
 SPACING = 1.5
@@ -31,9 +32,10 @@
     sectors, tiles, gather_rotation,
     snap_ref, dens_ref, speed_ref, off_ref, rot_ref,
     out_ref,
-    dens_in, speed_in, off_in, pad, rows, weighted, fields, rot_all, part, core_in, x_out, x_in, own, slots, far,
-    load_sem, cell_sem, own_rot_sem, halo_send, halo_recv, rot_send, rot_recv, core_send, core_recv, x_send, x_recv,
-    rs_send, rs_recv, far_send, far_recv, ag_send, ag_recv, agx_send, agx_recv, agc_send, agc_recv,
+    dens_in, speed_in, off_in, pad, rows, weighted, fields, rot_all, part, core_in, first_out, first_in, own, half_in, slots, far,
+    load_sem, cell_sem, own_rot_sem, halo_send, halo_recv, rot_send, rot_recv, core_send, core_recv, first_send, first_recv,
+    half_send, half_recv, rs_send, rs_recv, far_send, far_recv, ag_send, ag_recv,
+    back_half_send, back_half_recv, back_first_send, back_first_recv, agc_send, agc_recv,
 ):
     comps, cells, snaps = snap_ref.shape
     chunks = snaps // CHUNK
@@ -47,12 +49,15 @@
     side = s // 2
     low = lax.rem(t, GROUP)
     high = t // GROUP
-    comp = 2 * core + side
+    near = lax.rem(low, 2)
+    level = low // 2
     other_core = (s + 1 - 2 * core, t)
     other_side = (lax.rem(s + 2, sectors), t)
 
-    def group_tile(step):
-        return high * GROUP + lax.rem(low + step, GROUP)
+    other_near = (s, t + 1 - 2 * near)
+
+    def level_tile(step):
+        return high * GROUP + 2 * lax.rem(level + step, DEEP) + near
 
     def far_tile(step):
         return lax.rem(high + step, groups) * GROUP + low
@@ -80,7 +85,10 @@
         load.start()
 
     peers = [left, right, other_core, other_side]
-    peers += [(s, group_tile(d)) for d in range(1, GROUP)]
+    if gather_rotation:
+        peers += [(s, lax.rem(t + d, tiles)) for d in range(1, tiles)]
+    else:
+        peers += [other_near] + [(s, level_tile(d)) for d in range(1, DEEP)]
     peers += [(s, far_tile(e)) for e in range(1, groups)]
     barrier = pltpu.get_barrier_semaphore()
     for peer in peers:
@@ -186,8 +194,25 @@
     def span(q):
         return pl.ds(q * CHUNK, CHUNK)
 
-    def shard(q, lo):
-        return pl.ds(pl.multiple_of(q * CHUNK + lo * share, share), share)
+    half = CHUNK // 2
+
+    def bits(q):
+        return (side, near) if q % 2 == 0 else (near, side)
+
+    def partners(q):
+        return (other_side, other_near) if q % 2 == 0 else (other_near, other_side)
+
+    def kept(q):
+        return 2 * core + bits(q)[0]
+
+    def given(q):
+        return 2 * core + 1 - bits(q)[0]
+
+    def half_span(bit, base=0):
+        return pl.ds(pl.multiple_of(base + bit * half, share), half)
+
+    def shard(q, z, base=0):
+        return pl.ds(pl.multiple_of(base + bits(q)[1] * half + z * share, share), share)
 
     def core_copy(q):
         return remote(
@@ -195,14 +220,21 @@
             core_send.at[q], core_recv.at[q], other_core,
         )
 
-    def x_copy(q):
-        return remote(x_out.at[q], x_in.at[q], x_send.at[q], x_recv.at[q], other_side)
+    def first_copy(q):
+        return remote(
+            first_out.at[q], first_in.at[q], first_send.at[q], first_recv.at[q], partners(q)[0]
+        )
+
+    def half_copy(q):
+        return remote(
+            own.at[q, half_span(1 - bits(q)[1])], half_in.at[q],
+            half_send.at[q], half_recv.at[q], partners(q)[1],
+        )
 
     def rs_copy(q, d):
-        lo = lax.rem(low + d, GROUP)
-        return remote(
-            own.at[q, pl.ds(pl.multiple_of(lo * share, share), share)], slots.at[q, d],
-            rs_send.at[q, d], rs_recv.at[q, d], (s, group_tile(d)),
+        return remote(
+            own.at[q, shard(q, lax.rem(level + d, DEEP))], slots.at[q, d],
+            rs_send.at[q, d], rs_recv.at[q, d], (s, level_tile(d)),
         )
 
     def far_copy(q, e):
@@ -211,16 +243,24 @@
             far_send.at[q, e], far_recv.at[q, e], (s, far_tile(e)),
         )
 
-    def ag_copy(q, d):
-        place = out_ref.at[comp, shard(q, low)]
-        return remote(place, place, ag_send.at[q, d], ag_recv.at[q, d], (s, group_tile(d)))
-
-    def agx_copy(q):
-        place = out_ref.at[comp, span(q)]
-        return remote(place, place, agx_send.at[q], agx_recv.at[q], other_side)
-
-    def agc_copy(q):
-        place = out_ref.at[pl.ds(2 * core, 2), span(q)]
+    def ag_copy(q, d, z):
+        place = out_ref.at[kept(q), shard(q, z, q * CHUNK)]
+        return remote(place, place, ag_send.at[q, d], ag_recv.at[q, d], (s, level_tile(d)))
+
+    def back_half_copy(q, bit):
+        place = out_ref.at[kept(q), half_span(bit, q * CHUNK)]
+        return remote(
+            place, place, back_half_send.at[q], back_half_recv.at[q], partners(q)[1]
+        )
+
+    def back_first_copy(q, c):
+        place = out_ref.at[c, span(q)]
+        return remote(
+            place, place, back_first_send.at[q], back_first_recv.at[q], partners(q)[0]
+        )
+
+    def agc_copy(q, pair):
+        place = out_ref.at[pl.ds(2 * pair, 2), span(q)]
         return remote(place, place, agc_send.at[q], agc_recv.at[q], other_core)
 
     def begin(copy):
@@ -242,21 +282,28 @@
 
     def over_core(q):
         core_copy(q).wait_recv()
-        x_out[q] = part[2 * core + 1 - side, q * CHUNK : (q + 1) * CHUNK, :] + core_in[q, 1 - side]
-        begin(x_copy(q))
-        own[q] = part[comp, q * CHUNK : (q + 1) * CHUNK, :] + core_in[q, side]
-
-    def over_side(q):
-        x_copy(q).wait_recv()
-        own[q] = own[q] + x_in[q]
-        for d in range(1, GROUP):
+        bit = bits(q)[0]
+        first_out[q] = part[given(q), q * CHUNK : (q + 1) * CHUNK, :] + core_in[q, 1 - bit]
+        begin(first_copy(q))
+        own[q] = part[kept(q), q * CHUNK : (q + 1) * CHUNK, :] + core_in[q, bit]
+
+    def over_first(q):
+        first_copy(q).wait_recv()
+        own[q] = own[q] + first_in[q]
+        begin(half_copy(q))
+
+    def over_half(q):
+        half_copy(q).wait_recv()
+        mine = half_span(bits(q)[1])
+        own[q, mine, :] = own[q, mine, :] + half_in[q]
+        for d in range(1, DEEP):
             begin(rs_copy(q, d))
 
-    def over_tiles(q):
-        for d in range(1, GROUP):
+    def over_levels(q):
+        for d in range(1, DEEP):
             rs_copy(q, d).wait_recv()
-        value = own[q, pl.ds(pl.multiple_of(low * share, share), share), :]
-        for d in range(1, GROUP):
+        value = own[q, shard(q, level), :]
+        for d in range(1, DEEP):
             value = value + slots[q, d]
         if groups > 1:
             far[q, high] = value
@@ -271,29 +318,31 @@
             value = far[q, 0]
             for e in range(1, groups):
                 value = value + far[q, e]
-        out_ref[comp, shard(q, low), :] = value / math.sqrt(cell_total)
-        for d in range(1, GROUP):
-            begin(ag_copy(q, d))
-
-    def back_side(q):
-        for d in range(1, GROUP):
-            place = out_ref.at[comp, shard(q, lax.rem(low + GROUP - d, GROUP))]
-            remote(
-                place, place, ag_send.at[q, d], ag_recv.at[q, d], (s, group_tile(d))
-            ).wait_recv()
-        begin(agx_copy(q))
-
-    def back_core(q):
-        place = out_ref.at[2 * core + 1 - side, span(q)]
-        remote(place, place, agx_send.at[q], agx_recv.at[q], other_side).wait_recv()
-        begin(agc_copy(q))
+        out_ref[kept(q), shard(q, level, q * CHUNK), :] = value / math.sqrt(cell_total)
+        for d in range(1, DEEP):
+            begin(ag_copy(q, d, level))
+
+    def back_levels(q):
+        for d in range(1, DEEP):
+            ag_copy(q, d, lax.rem(level + DEEP - d, DEEP)).wait_recv()
+        begin(back_half_copy(q, bits(q)[1]))
+
+    def back_half(q):
+        back_half_copy(q, 1 - bits(q)[1]).wait_recv()
+        begin(back_first_copy(q, kept(q)))
+
+    def back_first(q):
+        back_first_copy(q, given(q)).wait_recv()
+        begin(agc_copy(q, core))
 
     def finish(q):
-        place = out_ref.at[pl.ds(2 * (1 - core), 2), span(q)]
-        remote(place, place, agc_send.at[q], agc_recv.at[q], other_core).wait_recv()
-
-    stages = [project, over_core, over_side, over_tiles, back_side, back_core, finish]
-    expected = (0.0, 1.2, 3.5, 6.8, 10.1, 12.4, 13.6)
+        agc_copy(q, 1 - core).wait_recv()
+
+    stages = [
+        project, over_core, over_first, over_half, over_levels,
+        back_levels, back_half, back_first, finish,
+    ]
+    expected = (0.0, 1.2, 3.2, 4.9, 7.0, 9.1, 10.8, 12.8, 14.0)
     for _, q, index in sorted(
         (SPACING * q + expected[index], q, index)
         for q in range(chunks)
@@ -337,7 +386,8 @@
             pltpu.VMEM((chunks, CHUNK, modes), f32),
             pltpu.VMEM((chunks, CHUNK, modes), f32),
             pltpu.VMEM((chunks, CHUNK, modes), f32),
-            pltpu.VMEM((chunks, GROUP, share, modes), f32),
+            pltpu.VMEM((chunks, CHUNK // 2, modes), f32),
+            pltpu.VMEM((chunks, DEEP, share, modes), f32),
             pltpu.VMEM((chunks, groups, share, modes), f32),
             dma((comps,)),
             dma((3,)),
@@ -350,12 +400,16 @@
             dma((chunks,)),
             dma((chunks,)),
             dma((chunks,)),
-            dma((chunks, GROUP)),
-            dma((chunks, GROUP)),
+            dma((chunks,)),
+            dma((chunks,)),
+            dma((chunks, DEEP)),
+            dma((chunks, DEEP)),
             dma((chunks, groups)),
             dma((chunks, groups)),
-            dma((chunks, GROUP)),
-            dma((chunks, GROUP)),
+            dma((chunks, DEEP)),
+            dma((chunks, DEEP)),
+            dma((chunks,)),
+            dma((chunks,)),
             dma((chunks,)),
             dma((chunks,)),
             dma((chunks,)),

time: 40.7 us -> 44.6 us (1.096)
  Pallas kernels: 38.5 us -> 42.3 us
    pallas_call x1, Pallas kernels: 38.5 us -> 42.3 us  [on_device(): pl.pallas_call(functools.partial(kernel, sectors, tiles, gather_rotation)...]
where the time goes in v4:
time: 44.6 us; the launch traced here: 44.4 us
  Pallas kernels  42.3 us (95%)
  local copies, waits for them, and re-layouts  2.06 us (5%)
    pallas_call x1, Pallas kernels, on_device(): pl.pallas_call(functools.partial(kernel, sectors, tiles, gather_rotation)...  42.3 us
    unnamed x1, local copies, waits for them, and re-layouts  2.06 us

profile of v4, /device:TPU:1, one launch (start us, length us, event | category | flops | bytes accessed | tf_op | source)
XLA Modules:
  0.0 44.4 jit_solution(2901446252664946162)
XLA Ops:
  0.0 42.3 %shard_map.55 = f32[4,384,128]{2,1,0:T(8,128)} custom-call(bf16[4,960,384]{2,1,0:T(8,128)(2,1)} %snap_ref.1, f32[1,960]{1,0:T(1,128)} %bitcast.3, f32[1,960]{1,0:T(1,128)} %bitcast.4, s32[1,960]{1,0:T(1,128)} %bitcast.5, bf16[48,128]{1,0:T(8,128)(2,1)} %rot_ref.1), custom_call_target="tpu_custom_call" | custom-call | flops 754974720 | bytes 2949120 | tf_op jit(solution)/shard_map/pallas_call | solution.py:370
  42.3 2.1 %copy.7 = f32[4,384,128]{2,1,0:T(8,128)} copy(f32[4,384,128]{2,1,0:T(8,128)} %shard_map.55) | data formatting | bytes 1572864

commit v5 on v2

--- a/solution.py
+++ b/solution.py
@@ -31,9 +31,9 @@
     sectors, tiles, gather_rotation,
     snap_ref, dens_ref, speed_ref, off_ref, rot_ref,
     out_ref,
-    dens_in, speed_in, off_in, pad, rows, weighted, fields, rot_all, part, core_in, x_out, x_in, own, slots, far,
-    load_sem, cell_sem, own_rot_sem, halo_send, halo_recv, rot_send, rot_recv, core_send, core_recv, x_send, x_recv,
-    rs_send, rs_recv, far_send, far_recv, ag_send, ag_recv, agx_send, agx_recv, agc_send, agc_recv,
+    dens_in, speed_in, off_in, pad, rows, weighted, fields, rot_all, part, core_in, own, slots, far,
+    load_sem, cell_sem, own_rot_sem, halo_send, halo_recv, rot_send, rot_recv, core_send, core_recv,
+    rs_send, rs_recv, far_send, far_recv, ag_send, ag_recv, agc_send, agc_recv,
 ):
     comps, cells, snaps = snap_ref.shape
     chunks = snaps // CHUNK
@@ -54,6 +54,10 @@
     def group_tile(step):
         return high * GROUP + lax.rem(low + step, GROUP)
 
+    def holder(step):
+        sector = s if step < GROUP else lax.rem(s + 2, sectors)
+        return (sector, group_tile(step % GROUP))
+
     def far_tile(step):
         return lax.rem(high + step, groups) * GROUP + low
 
@@ -81,6 +85,7 @@
 
     peers = [left, right, other_core, other_side]
     peers += [(s, group_tile(d)) for d in range(1, GROUP)]
+    peers += [holder(GROUP + d) for d in range(1, GROUP)]
     peers += [(s, far_tile(e)) for e in range(1, groups)]
     barrier = pltpu.get_barrier_semaphore()
     for peer in peers:
@@ -195,14 +200,12 @@
             core_send.at[q], core_recv.at[q], other_core,
         )
 
-    def x_copy(q):
-        return remote(x_out.at[q], x_in.at[q], x_send.at[q], x_recv.at[q], other_side)
-
     def rs_copy(q, d):
         lo = lax.rem(low + d, GROUP)
+        slab = side if d < GROUP else 1 - side
         return remote(
-            own.at[q, pl.ds(pl.multiple_of(lo * share, share), share)], slots.at[q, d],
-            rs_send.at[q, d], rs_recv.at[q, d], (s, group_tile(d)),
+            own.at[q, slab, pl.ds(pl.multiple_of(lo * share, share), share)], slots.at[q, d],
+            rs_send.at[q, d], rs_recv.at[q, d], holder(d),
         )
 
     def far_copy(q, e):
@@ -211,13 +214,9 @@
             far_send.at[q, e], far_recv.at[q, e], (s, far_tile(e)),
         )
 
-    def ag_copy(q, d):
-        place = out_ref.at[comp, shard(q, low)]
-        return remote(place, place, ag_send.at[q, d], ag_recv.at[q, d], (s, group_tile(d)))
-
-    def agx_copy(q):
-        place = out_ref.at[comp, span(q)]
-        return remote(place, place, agx_send.at[q], agx_recv.at[q], other_side)
+    def ag_copy(q, d, c, lo):
+        place = out_ref.at[c, shard(q, lo)]
+        return remote(place, place, ag_send.at[q, d], ag_recv.at[q, d], holder(d))
 
     def agc_copy(q):
         place = out_ref.at[pl.ds(2 * core, 2), span(q)]
@@ -242,21 +241,15 @@
 
     def over_core(q):
         core_copy(q).wait_recv()
-        x_out[q] = part[2 * core + 1 - side, q * CHUNK : (q + 1) * CHUNK, :] + core_in[q, 1 - side]
-        begin(x_copy(q))
-        own[q] = part[comp, q * CHUNK : (q + 1) * CHUNK, :] + core_in[q, side]
-
-    def over_side(q):
-        x_copy(q).wait_recv()
-        own[q] = own[q] + x_in[q]
-        for d in range(1, GROUP):
+        own[q] = part[pl.ds(2 * core, 2), q * CHUNK : (q + 1) * CHUNK, :] + core_in[q]
+        for d in range(1, 2 * GROUP):
             begin(rs_copy(q, d))
 
     def over_tiles(q):
-        for d in range(1, GROUP):
+        for d in range(1, 2 * GROUP):
             rs_copy(q, d).wait_recv()
-        value = own[q, pl.ds(pl.multiple_of(low * share, share), share), :]
-        for d in range(1, GROUP):
+        value = own[q, side, pl.ds(pl.multiple_of(low * share, share), share), :]
+        for d in range(1, 2 * GROUP):
             value = value + slots[q, d]
         if groups > 1:
             far[q, high] = value
@@ -272,28 +265,21 @@
             for e in range(1, groups):
                 value = value + far[q, e]
         out_ref[comp, shard(q, low), :] = value / math.sqrt(cell_total)
-        for d in range(1, GROUP):
-            begin(ag_copy(q, d))
-
-    def back_side(q):
-        for d in range(1, GROUP):
-            place = out_ref.at[comp, shard(q, lax.rem(low + GROUP - d, GROUP))]
-            remote(
-                place, place, ag_send.at[q, d], ag_recv.at[q, d], (s, group_tile(d))
-            ).wait_recv()
-        begin(agx_copy(q))
+        for d in range(1, 2 * GROUP):
+            begin(ag_copy(q, d, comp, low))
 
     def back_core(q):
-        place = out_ref.at[2 * core + 1 - side, span(q)]
-        remote(place, place, agx_send.at[q], agx_recv.at[q], other_side).wait_recv()
+        for d in range(1, 2 * GROUP):
+            source = comp if d < GROUP else 2 * core + 1 - side
+            ag_copy(q, d, source, lax.rem(low + GROUP - d % GROUP, GROUP)).wait_recv()
         begin(agc_copy(q))
 
     def finish(q):
         place = out_ref.at[pl.ds(2 * (1 - core), 2), span(q)]
         remote(place, place, agc_send.at[q], agc_recv.at[q], other_core).wait_recv()
 
-    stages = [project, over_core, over_side, over_tiles, back_side, back_core, finish]
-    expected = (0.0, 1.2, 3.5, 6.8, 10.1, 12.4, 13.6)
+    stages = [project, over_core, over_tiles, back_core, finish]
+    expected = (0.0, 1.3, 6.0, 11.0, 12.3)
     for _, q, index in sorted(
         (SPACING * q + expected[index], q, index)
         for q in range(chunks)
@@ -334,10 +320,8 @@
             pltpu.VMEM((snaps, modes), bf16),
             pltpu.VMEM((comps, snaps, modes), f32),
             pltpu.VMEM((chunks, 2, CHUNK, modes), f32),
-            pltpu.VMEM((chunks, CHUNK, modes), f32),
-            pltpu.VMEM((chunks, CHUNK, modes), f32),
-            pltpu.VMEM((chunks, CHUNK, modes), f32),
-            pltpu.VMEM((chunks, GROUP, share, modes), f32),
+            pltpu.VMEM((chunks, 2, CHUNK, modes), f32),
+            pltpu.VMEM((chunks, 2 * GROUP, share, modes), f32),
             pltpu.VMEM((chunks, groups, share, modes), f32),
             dma((comps,)),
             dma((3,)),
@@ -348,16 +332,12 @@
             dma((tiles,)),
             dma((chunks,)),
             dma((chunks,)),
-            dma((chunks,)),
-            dma((chunks,)),
-            dma((chunks, GROUP)),
-            dma((chunks, GROUP)),
+            dma((chunks, 2 * GROUP)),
+            dma((chunks, 2 * GROUP)),
             dma((chunks, groups)),
             dma((chunks, groups)),
-            dma((chunks, GROUP)),
-            dma((chunks, GROUP)),
-            dma((chunks,)),
-            dma((chunks,)),
+            dma((chunks, 2 * GROUP)),
+            dma((chunks, 2 * GROUP)),
             dma((chunks,)),
             dma((chunks,)),
         ],

time: 40.7 us -> 40.4 us (level)
  Pallas kernels: 38.5 us -> 38 us
    pallas_call x1, Pallas kernels: 38.5 us -> 38 us  [on_device(): pl.pallas_call(functools.partial(kernel, sectors, tiles, gather_rotation)...]
where the time goes in v5:
time: 40.4 us; the launch traced here: 40.1 us
  Pallas kernels  38 us (94%)
  local copies, waits for them, and re-layouts  2.06 us (5%)
    pallas_call x1, Pallas kernels, on_device(): pl.pallas_call(functools.partial(kernel, sectors, tiles, gather_rotation)...  38 us
    unnamed x1, local copies, waits for them, and re-layouts  2.06 us

profile of v5, /device:TPU:1, one launch (start us, length us, event | category | flops | bytes accessed | tf_op | source)
XLA Modules:
  0.0 40.1 jit_solution(2395265852557496026)
XLA Ops:
  0.0 38.0 %shard_map.55 = f32[4,384,128]{2,1,0:T(8,128)} custom-call(bf16[4,960,384]{2,1,0:T(8,128)(2,1)} %snap_ref.1, f32[1,960]{1,0:T(1,128)} %bitcast.3, f32[1,960]{1,0:T(1,128)} %bitcast.4, s32[1,960]{1,0:T(1,128)} %bitcast.5, bf16[48,128]{1,0:T(8,128)(2,1)} %rot_ref.1), custom_call_target="tpu_custom_call" | custom-call | flops 754974720 | bytes 2949120 | tf_op jit(solution)/shard_map/pallas_call | solution.py:307
  38.0 2.1 %copy.7 = f32[4,384,128]{2,1,0:T(8,128)} copy(f32[4,384,128]{2,1,0:T(8,128)} %shard_map.55) | data formatting | bytes 1572864

commit v6 on v5

--- a/solution.py
+++ b/solution.py
@@ -167,8 +167,9 @@
     for load in loads:
         load.wait()
     blocks = cells // BLOCK
-    for block in range(1, blocks - 1):
-        weigh(block, 0)
+    for q in range(chunks):
+        for block in range(1, blocks - 1):
+            weigh(block, q)
 
     if gather_rotation:
         for d in range(1, tiles):
@@ -228,8 +229,8 @@
 
     def project(q):
         if q > 0:
-            for block in range(blocks):
-                weigh(block, q)
+            weigh(0, q)
+            weigh(blocks - 1, q)
         for c in range(comps):
             part[c, q * CHUNK : (q + 1) * CHUNK, :] = lax.dot_general(
                 weighted[c, :, q * CHUNK : (q + 1) * CHUNK],

time: 40.4 us -> 41.3 us (1.022)
  Pallas kernels: 38 us -> 39.1 us
    pallas_call x1, Pallas kernels: 38 us -> 39.1 us  [on_device(): pl.pallas_call(functools.partial(kernel, sectors, tiles, gather_rotation)...]
where the time goes in v6:
time: 41.3 us; the launch traced here: 41.2 us
  Pallas kernels  39.1 us (95%)
  local copies, waits for them, and re-layouts  2.06 us (5%)
    pallas_call x1, Pallas kernels, on_device(): pl.pallas_call(functools.partial(kernel, sectors, tiles, gather_rotation)...  39.1 us
    unnamed x1, local copies, waits for them, and re-layouts  2.06 us

profile of v6, /device:TPU:1, one launch (start us, length us, event | category | flops | bytes accessed | tf_op | source)
XLA Modules:
  0.0 41.2 jit_solution(2046732797642201502)
XLA Ops:
  0.0 39.1 %shard_map.55 = f32[4,384,128]{2,1,0:T(8,128)} custom-call(bf16[4,960,384]{2,1,0:T(8,128)(2,1)} %snap_ref.1, f32[1,960]{1,0:T(1,128)} %bitcast.3, f32[1,960]{1,0:T(1,128)} %bitcast.4, s32[1,960]{1,0:T(1,128)} %bitcast.5, bf16[48,128]{1,0:T(8,128)(2,1)} %rot_ref.1), custom_call_target="tpu_custom_call" | custom-call | flops 754974720 | bytes 2949120 | tf_op jit(solution)/shard_map/pallas_call | solution.py:308
  39.1 2.1 %copy.7 = f32[4,384,128]{2,1,0:T(8,128)} copy(f32[4,384,128]{2,1,0:T(8,128)} %shard_map.55) | data formatting | bytes 1572864
